TPU v7x, 32 devices: a whole 2x2x4 slice. The times are simulated.
32 devices in a mesh: tm: 8 (over z, x), chan: 4 (over y, core).
Axes of the slice: x: 2, y: 2, z: 4, core: 2. Of those that a mesh axis runs over, the one named last changes fastest.
Arguments:
- inputs: bfloat16 [16, 256, 512], P('tm'), may hold values from -6 to 6
- decay: float32 [16, 512], P('tm', 'chan'), may hold values from 0 to 1, as said below
- kernel_b: bfloat16 [9, 512, 256], P(None, 'chan'), may hold values from -0.125 to 0.125
- kernel_c: bfloat16 [9, 256, 512], P(None, 'chan'), may hold values from -0.09375 to 0.09375
- cotangent: bfloat16 [16, 256, 512], P('tm', 'chan'), may hold values from -0.0625 to 0.0625
Outputs:
- grad_b: float32 [9, 512, 256], P(None, 'chan')
- grad_c: float32 [9, 256, 512], P(None, 'chan')
- decay_grad: float32 [16, 512], P('tm', 'chan')
Inputs may be any that keep to these rules, and one draw needn't show every extreme that they name: decay lies strictly between 0 and 1.
All inputs are finite; a program needn't handle non-finite values.
Results may differ from a plain program's by a relative error of at most 0.003.
Values may be sent and summed in bfloat16 or wider, within the bound.
A program may use at most 128 MiB of HBM per device.

v0:
```python
import jax
import jax.numpy as jnp
from jax import lax
from jax.sharding import PartitionSpec as P

W = 64


offsets = ((-1, -1), (-1, 0), (-1, 1), (0, -1), (0, 0), (0, 1), (1, -1), (1, 0), (1, 1))


def passed_along(value, axis, steps):
    count = lax.axis_size(axis)
    first, last = (max(0, -steps), min(count, count - steps))
    return lax.ppermute(value, axis, [(source, source + steps) for source in range(first, last)])


def shift_cells(source, row_shift, col_shift, grid_width):
    cell_count = source.shape[-1]
    margin = grid_width + 1
    padded = jnp.pad(source, [(0, 0)] * (source.ndim - 1) + [(margin, margin)])
    first_cell = margin + row_shift * grid_width + col_shift
    shifted = lax.slice_in_dim(padded, first_cell, first_cell + cell_count, axis=source.ndim - 1)
    column = jnp.arange(cell_count) % grid_width
    inside = (column + col_shift >= 0) & (column + col_shift < grid_width)
    return jnp.where(inside, shifted, jnp.zeros((), source.dtype))


def stencil_stack(source, grid_width, decay_factor):
    parts = [
        shift_cells(source, decay_factor * pair[0], decay_factor * pair[1], grid_width)
        for pair in offsets
    ]
    return jnp.stack(parts, axis=source.ndim - 2)


def body(inputs, decay, kernel_b, kernel_c, cotangent):
    local_rows = kernel_b.shape[1]
    cell_count = inputs.shape[-1]
    blank_state = jnp.zeros((local_rows, cell_count), jnp.float32)
    input_stack = stencil_stack(inputs, W, 1)
    drives = jnp.einsum("kpc,fkcs->fps", kernel_b, input_stack, preferred_element_type=jnp.float32)

    def advance(current, frame_pair):
        frame_rate, drive = frame_pair
        current = frame_rate[:, None] * current + drive
        return (current, current)

    local_end, local_states = lax.scan(advance, blank_state, (decay, drives))
    decay_total = jnp.prod(decay, axis=0)

    def relay_state(turn_index, carried):
        outgoing = decay_total[:, None] * carried + local_end
        return passed_along(outgoing, "tm", 1)

    entering = lax.fori_loop(0, lax.axis_size("tm") - 1, relay_state, blank_state)
    cumulative = jnp.cumprod(decay, axis=0)
    states = local_states + cumulative[:, :, None] * entering[None]
    previous = jnp.concatenate([entering[None], states[:-1]], axis=0)
    states_bf = states.astype(jnp.bfloat16)
    cot_stack = stencil_stack(cotangent, W, -1)
    injected = lax.psum_scatter(
        jnp.einsum("kup,fkus->pfs", kernel_c, cot_stack, preferred_element_type=jnp.float32),
        "chan",
        scatter_dimension=0,
        tiled=True,
    )
    injected = jnp.moveaxis(injected, 1, 0)

    def retreat(carried, frame_pair):
        frame_rate, source = frame_pair
        adjoint = source + carried
        return (frame_rate[:, None] * adjoint, adjoint)

    message, local_adjoint = lax.scan(retreat, blank_state, (decay, injected), reverse=True)

    def relay_adjoint(turn_index, carried):
        outgoing = decay_total[:, None] * carried + message
        return passed_along(outgoing, "tm", -1)

    arriving = lax.fori_loop(0, lax.axis_size("tm") - 1, relay_adjoint, blank_state)
    suffix = jnp.flip(jnp.cumprod(jnp.flip(decay, 0), 0), 0)
    later_decay = jnp.concatenate([suffix[1:], jnp.ones_like(decay[:1])], axis=0)
    adjoint = local_adjoint + later_decay[:, :, None] * arriving[None]
    decay_grad = jnp.sum(adjoint * previous, axis=2)
    adjoint_bf = adjoint.astype(jnp.bfloat16)
    grad_b_part = jnp.einsum(
        "fps,fkcs->kpc", adjoint_bf, input_stack, preferred_element_type=jnp.float32
    )
    shifted = stencil_stack(lax.all_gather(states_bf, "chan", axis=1, tiled=True), W, 1)
    grad_c_part = jnp.einsum(
        "fus,fkps->kup", cotangent, shifted, preferred_element_type=jnp.float32
    )
    grad_b, grad_c = lax.psum((grad_b_part, grad_c_part), "tm")
    return (grad_b, grad_c, decay_grad)


def solution(mesh):
    in_specs = (
        P("tm", None, None),
        P("tm", "chan"),
        P(None, "chan", None),
        P(None, "chan", None),
        P("tm", "chan", None),
    )
    out_specs = (P(None, "chan", None), P(None, "chan", None), P("tm", "chan"))
    return jax.shard_map(body, mesh=mesh, in_specs=in_specs, out_specs=out_specs, check_vma=False)
```

profile of v0, /device:TPU:15, one launch (start us, length us, event | category | flops | bytes accessed | tf_op | source)
XLA Modules:
  0.0 335.5 jit_solution(1531340862124081338)
XLA Ops:
  20.7 59.3 %while.51 = (s32[]{:T(128)}, f32[128,512]{1,0:T(8,128)S(1)}, f32[128]{0:T(128)S(1)}, f32[128,512]{1,0:T(8,128)S(1)}, s32[]{:T(128)}) while((s32[]{:T(128)}, f32[128,512]{1,0:T(8,128)S(1)}, f32[128]{0:T(128)S(1)}, f32[128,512]{1,0:T(8,128)S(1)}, s32[]{:T(128)}) %tuple.101), condition=%wide.region_12.13_spmd, body=%wide.region_11.12_spmd.sunk | while | flops 131074 | bytes 1835621 | solution.py:56
  24.0 5.9 %collective-permute-done.1 = f32[128,512]{1,0:T(8,128)S(1)} collective-permute-done((f32[128,512]{1,0:T(8,128)S(1)}, f32[128,512]{1,0:T(8,128)S(1)}, u32[]{:S(2)}, u32[]{:S(2)}) %collective-permute-start.1) | collective-permute-done | bytes 262176 | tf_op jit(solution)/shard_map/while/body/eval_jaxpr/ppermute | solution.py:15
  29.9 4.1 %collective-permute-start.1 = (f32[128,512]{1,0:T(8,128)S(1)}, f32[128,512]{1,0:T(8,128)S(1)}, u32[]{:S(2)}, u32[]{:S(2)}) collective-permute-start(f32[128,512]{1,0:T(8,128)S(1)} %multiply_add_fusion.8), channel_id=1, source_target_pairs={{0,4},{4,8},{8,12},{12,16},{16,20},{20,24},{24,28},{1,5},{5,9},{9,... | collective-permute-start | bytes 786440 | tf_op jit(solution)/shard_map/while/body/eval_jaxpr/ppermute | solution.py:15
  34.0 4.1 %collective-permute-done.1 = f32[128,512]{1,0:T(8,128)S(1)} collective-permute-done((f32[128,512]{1,0:T(8,128)S(1)}, f32[128,512]{1,0:T(8,128)S(1)}, u32[]{:S(2)}, u32[]{:S(2)}) %collective-permute-start.1) | collective-permute-done | bytes 262176 | tf_op jit(solution)/shard_map/while/body/eval_jaxpr/ppermute | solution.py:15
  38.2 5.0 %collective-permute-start.1 = (f32[128,512]{1,0:T(8,128)S(1)}, f32[128,512]{1,0:T(8,128)S(1)}, u32[]{:S(2)}, u32[]{:S(2)}) collective-permute-start(f32[128,512]{1,0:T(8,128)S(1)} %multiply_add_fusion.8), channel_id=1, source_target_pairs={{0,4},{4,8},{8,12},{12,16},{16,20},{20,24},{24,28},{1,5},{5,9},{9,... | collective-permute-start | bytes 786440 | tf_op jit(solution)/shard_map/while/body/eval_jaxpr/ppermute | solution.py:15
  43.2 3.3 collective-permute-done.1
  46.5 4.7 %collective-permute-start.1 = (f32[128,512]{1,0:T(8,128)S(1)}, f32[128,512]{1,0:T(8,128)S(1)}, u32[]{:S(2)}, u32[]{:S(2)}) collective-permute-start(f32[128,512]{1,0:T(8,128)S(1)} %multiply_add_fusion.8), channel_id=1, source_target_pairs={{0,4},{4,8},{8,12},{12,16},{16,20},{20,24},{24,28},{1,5},{5,9},{9,... | collective-permute-start | bytes 786440 | tf_op jit(solution)/shard_map/while/body/eval_jaxpr/ppermute | solution.py:15
  54.6 4.7 %collective-permute-start.1 = (f32[128,512]{1,0:T(8,128)S(1)}, f32[128,512]{1,0:T(8,128)S(1)}, u32[]{:S(2)}, u32[]{:S(2)}) collective-permute-start(f32[128,512]{1,0:T(8,128)S(1)} %multiply_add_fusion.8), channel_id=1, source_target_pairs={{0,4},{4,8},{8,12},{12,16},{16,20},{20,24},{24,28},{1,5},{5,9},{9,... | collective-permute-start | bytes 786440 | tf_op jit(solution)/shard_map/while/body/eval_jaxpr/ppermute | solution.py:15
  62.8 4.7 %collective-permute-start.1 = (f32[128,512]{1,0:T(8,128)S(1)}, f32[128,512]{1,0:T(8,128)S(1)}, u32[]{:S(2)}, u32[]{:S(2)}) collective-permute-start(f32[128,512]{1,0:T(8,128)S(1)} %multiply_add_fusion.8), channel_id=1, source_target_pairs={{0,4},{4,8},{8,12},{12,16},{16,20},{20,24},{24,28},{1,5},{5,9},{9,... | collective-permute-start | bytes 786440 | tf_op jit(solution)/shard_map/while/body/eval_jaxpr/ppermute | solution.py:15
  70.9 4.7 %collective-permute-start.1 = (f32[128,512]{1,0:T(8,128)S(1)}, f32[128,512]{1,0:T(8,128)S(1)}, u32[]{:S(2)}, u32[]{:S(2)}) collective-permute-start(f32[128,512]{1,0:T(8,128)S(1)} %multiply_add_fusion.8), channel_id=1, source_target_pairs={{0,4},{4,8},{8,12},{12,16},{16,20},{20,24},{24,28},{1,5},{5,9},{9,... | collective-permute-start | bytes 786440 | tf_op jit(solution)/shard_map/while/body/eval_jaxpr/ppermute | solution.py:15
  75.6 4.4 %collective-permute-done.1 = f32[128,512]{1,0:T(8,128)S(1)} collective-permute-done((f32[128,512]{1,0:T(8,128)S(1)}, f32[128,512]{1,0:T(8,128)S(1)}, u32[]{:S(2)}, u32[]{:S(2)}) %collective-permute-start.1) | collective-permute-done | bytes 262176 | tf_op jit(solution)/shard_map/while/body/eval_jaxpr/ppermute | solution.py:15
  84.6 21.7 %all-gather.2.cloned.1.call-done = bf16[2,512,512]{2,1,0:T(8,128)(2,1)} async-done(((bf16[2,128,512]{2,1,0:T(8,128)(2,1)}), bf16[2,512,512]{2,1,0:T(8,128)(2,1)}) %all-gather.2.cloned.1.call-update) | async-done | bytes 1048592 | tf_op jit(solution)/shard_map/all_gather | solution.py:90
  113.3 4.0 %convolution_bitcast_fusion.1 = f32[9,64,512]{2,1,0:T(8,128)} fusion(bf16[2,9,512,512]{3,2,0,1:T(8,128)(2,1)S(1)} %fusion.25, bf16[2,64,512]{2,1,0:T(8,128)(2,1)S(1)} %copy-done.3), kind=kOutput, calls=%fused_computation.23 | convolution fusion | flops 603979776 | bytes 10747904 | tf_op jit(solution)/shard_map/fus,fkps->kup/dot_general | solution.py:91
  117.3 22.7 %reduce-scatter.2.cloned.1.call-done = f32[128,2,512]{0,2,1:T(8,128)} async-done(((f32[512,2,512]{0,2,1:T(8,128)}), f32[128,2,512]{0,2,1:T(8,128)}) %reduce-scatter.2.cloned.1.call-update) | async-done | bytes 524304 | tf_op jit(solution)/shard_map/reduce_scatter | solution.py:62
  142.6 60.9 %while.50 = (s32[]{:T(128)}, f32[128,512]{1,0:T(8,128)S(1)}, f32[128]{0:T(128)S(1)}, f32[128,512]{1,0:T(8,128)S(1)}, s32[]{:T(128)}) while((s32[]{:T(128)}, f32[128,512]{1,0:T(8,128)S(1)}, f32[128]{0:T(128)S(1)}, f32[128,512]{1,0:T(8,128)S(1)}, s32[]{:T(128)}) %tuple.113), condition=%wide.region_6.7_spmd, body=%wide.region_5.6_spmd.sunk | while | flops 131074 | bytes 1835621 | solution.py:81
  144.9 7.8 %collective-permute-done = f32[128,512]{1,0:T(8,128)S(1)} collective-permute-done((f32[128,512]{1,0:T(8,128)S(1)}, f32[128,512]{1,0:T(8,128)S(1)}, u32[]{:S(2)}, u32[]{:S(2)}) %collective-permute-start) | collective-permute-done | bytes 262176 | tf_op jit(solution)/shard_map/while/body/eval_jaxpr/ppermute | solution.py:15
  154.7 7.1 %collective-permute-done = f32[128,512]{1,0:T(8,128)S(1)} collective-permute-done((f32[128,512]{1,0:T(8,128)S(1)}, f32[128,512]{1,0:T(8,128)S(1)}, u32[]{:S(2)}, u32[]{:S(2)}) %collective-permute-start) | collective-permute-done | bytes 262176 | tf_op jit(solution)/shard_map/while/body/eval_jaxpr/ppermute | solution.py:15
  163.9 6.1 %collective-permute-done = f32[128,512]{1,0:T(8,128)S(1)} collective-permute-done((f32[128,512]{1,0:T(8,128)S(1)}, f32[128,512]{1,0:T(8,128)S(1)}, u32[]{:S(2)}, u32[]{:S(2)}) %collective-permute-start) | collective-permute-done | bytes 262176 | tf_op jit(solution)/shard_map/while/body/eval_jaxpr/ppermute | solution.py:15
  172.0 6.1 %collective-permute-done = f32[128,512]{1,0:T(8,128)S(1)} collective-permute-done((f32[128,512]{1,0:T(8,128)S(1)}, f32[128,512]{1,0:T(8,128)S(1)}, u32[]{:S(2)}, u32[]{:S(2)}) %collective-permute-start) | collective-permute-done | bytes 262176 | tf_op jit(solution)/shard_map/while/body/eval_jaxpr/ppermute | solution.py:15
  180.1 6.1 %collective-permute-done = f32[128,512]{1,0:T(8,128)S(1)} collective-permute-done((f32[128,512]{1,0:T(8,128)S(1)}, f32[128,512]{1,0:T(8,128)S(1)}, u32[]{:S(2)}, u32[]{:S(2)}) %collective-permute-start) | collective-permute-done | bytes 262176 | tf_op jit(solution)/shard_map/while/body/eval_jaxpr/ppermute | solution.py:15
  188.2 6.1 %collective-permute-done = f32[128,512]{1,0:T(8,128)S(1)} collective-permute-done((f32[128,512]{1,0:T(8,128)S(1)}, f32[128,512]{1,0:T(8,128)S(1)}, u32[]{:S(2)}, u32[]{:S(2)}) %collective-permute-start) | collective-permute-done | bytes 262176 | tf_op jit(solution)/shard_map/while/body/eval_jaxpr/ppermute | solution.py:15
  196.3 7.2 %collective-permute-done = f32[128,512]{1,0:T(8,128)S(1)} collective-permute-done((f32[128,512]{1,0:T(8,128)S(1)}, f32[128,512]{1,0:T(8,128)S(1)}, u32[]{:S(2)}, u32[]{:S(2)}) %collective-permute-start) | collective-permute-done | bytes 262176 | tf_op jit(solution)/shard_map/while/body/eval_jaxpr/ppermute | solution.py:15
  203.5 4.8 %convolution_bitcast_fusion.2 = f32[9,128,256]{1,2,0:T(8,128)} fusion(bf16[2,9,256,512]{3,2,0,1:T(8,128)(2,1)} %copy-done.4, f32[2,128,512]{2,1,0:T(8,128)S(1)} %get-tuple-element.179, f32[128,512]{1,0:T(8,128)S(1)} %get-tuple-element.181, f32[2,128]{1,0:T(2,128)S(1)} %broadcast_select_fusion), kind=kOutput, calls=%fused_computation.24 | convolution fusion | flops 604372992 | bytes 6685696 | tf_op jit(solution)/shard_map/fps,fkcs->kpc/dot_general | solution.py:87
  209.1 114.8 %all-reduce.6.cloned.1.call-done = (f32[9,128,256]{1,2,0:T(8,128)}, f32[9,64,512]{2,1,0:T(8,128)}) async-done(((f32[9,128,256]{1,2,0:T(8,128)}, f32[9,64,512]{2,1,0:T(8,128)}), (f32[9,128,256]{1,2,0:T(8,128)}, f32[9,64,512]{2,1,0:T(8,128)})) %all-reduce.6.cloned.1.call-update) | async-done | bytes 2359312 | tf_op jit(solution)/shard_map/psum | solution.py:94
  (115 shorter events, 64.3 us)
Async XLA Ops:
  7.2 74.6 %copy-start = (bf16[9,64,512]{2,1,0:T(8,128)(2,1)S(1)}, bf16[9,64,512]{2,1,0:T(8,128)(2,1)}, u32[]{:S(2)}) copy-start(bf16[9,64,512]{2,1,0:T(8,128)(2,1)} %param.16) | copy-start | bytes 1769476
  7.2 8.1 %copy-start.2 = (bf16[2,256,512]{2,1,0:T(8,128)(2,1)S(1)}, bf16[2,256,512]{2,1,0:T(8,128)(2,1)}, u32[]{:S(2)}) copy-start(bf16[2,256,512]{2,1,0:T(8,128)(2,1)} %param.13) | copy-start | bytes 1572868
  7.2 99.2 %all-gather.2.cloned.1.call-start = ((), (), s32[]{:S(2)}) async-start(), calls=%async_computation.2 | async-start | bytes 1310720 | tf_op jit(solution)/shard_map/all_gather | solution.py:90
  8.8 9.7 %copy-start.7 = (bf16[9,128,256]{2,1,0:T(8,128)(2,1)S(1)}, bf16[9,128,256]{2,1,0:T(8,128)(2,1)}, u32[]{:S(2)}) copy-start(bf16[9,128,256]{2,1,0:T(8,128)(2,1)} %param.15) | copy-start | bytes 1769476
  16.4 2.1 copy-start.4
  20.6 60.2 %copy-start.3 = (bf16[2,64,512]{2,1,0:T(8,128)(2,1)S(1)}, bf16[2,64,512]{2,1,0:T(8,128)(2,1)}, u32[]{:S(2)}) copy-start(bf16[2,64,512]{2,1,0:T(8,128)(2,1)} %param.17) | copy-start | bytes 393220
  20.8 9.1 %collective-permute-start.1 = (f32[128,512]{1,0:T(8,128)S(1)}, f32[128,512]{1,0:T(8,128)S(1)}, u32[]{:S(2)}, u32[]{:S(2)}) collective-permute-start(f32[128,512]{1,0:T(8,128)S(1)} %multiply_add_fusion.8), channel_id=1, source_target_pairs={{0,4},{4,8},{8,12},{12,16},{16,20},{20,24},{24,28},{1,5},{5,9},{9,... | collective-permute-start | bytes 786440 | tf_op jit(solution)/shard_map/while/body/eval_jaxpr/ppermute | solution.py:15
  29.9 8.1 %collective-permute-start.1 = (f32[128,512]{1,0:T(8,128)S(1)}, f32[128,512]{1,0:T(8,128)S(1)}, u32[]{:S(2)}, u32[]{:S(2)}) collective-permute-start(f32[128,512]{1,0:T(8,128)S(1)} %multiply_add_fusion.8), channel_id=1, source_target_pairs={{0,4},{4,8},{8,12},{12,16},{16,20},{20,24},{24,28},{1,5},{5,9},{9,... | collective-permute-start | bytes 786440 | tf_op jit(solution)/shard_map/while/body/eval_jaxpr/ppermute | solution.py:15
  38.2 8.3 %collective-permute-start.1 = (f32[128,512]{1,0:T(8,128)S(1)}, f32[128,512]{1,0:T(8,128)S(1)}, u32[]{:S(2)}, u32[]{:S(2)}) collective-permute-start(f32[128,512]{1,0:T(8,128)S(1)} %multiply_add_fusion.8), channel_id=1, source_target_pairs={{0,4},{4,8},{8,12},{12,16},{16,20},{20,24},{24,28},{1,5},{5,9},{9,... | collective-permute-start | bytes 786440 | tf_op jit(solution)/shard_map/while/body/eval_jaxpr/ppermute | solution.py:15
  46.5 8.0 %collective-permute-start.1 = (f32[128,512]{1,0:T(8,128)S(1)}, f32[128,512]{1,0:T(8,128)S(1)}, u32[]{:S(2)}, u32[]{:S(2)}) collective-permute-start(f32[128,512]{1,0:T(8,128)S(1)} %multiply_add_fusion.8), channel_id=1, source_target_pairs={{0,4},{4,8},{8,12},{12,16},{16,20},{20,24},{24,28},{1,5},{5,9},{9,... | collective-permute-start | bytes 786440 | tf_op jit(solution)/shard_map/while/body/eval_jaxpr/ppermute | solution.py:15
  54.6 8.0 %collective-permute-start.1 = (f32[128,512]{1,0:T(8,128)S(1)}, f32[128,512]{1,0:T(8,128)S(1)}, u32[]{:S(2)}, u32[]{:S(2)}) collective-permute-start(f32[128,512]{1,0:T(8,128)S(1)} %multiply_add_fusion.8), channel_id=1, source_target_pairs={{0,4},{4,8},{8,12},{12,16},{16,20},{20,24},{24,28},{1,5},{5,9},{9,... | collective-permute-start | bytes 786440 | tf_op jit(solution)/shard_map/while/body/eval_jaxpr/ppermute | solution.py:15
  62.8 8.0 %collective-permute-start.1 = (f32[128,512]{1,0:T(8,128)S(1)}, f32[128,512]{1,0:T(8,128)S(1)}, u32[]{:S(2)}, u32[]{:S(2)}) collective-permute-start(f32[128,512]{1,0:T(8,128)S(1)} %multiply_add_fusion.8), channel_id=1, source_target_pairs={{0,4},{4,8},{8,12},{12,16},{16,20},{20,24},{24,28},{1,5},{5,9},{9,... | collective-permute-start | bytes 786440 | tf_op jit(solution)/shard_map/while/body/eval_jaxpr/ppermute | solution.py:15
  70.9 9.1 %collective-permute-start.1 = (f32[128,512]{1,0:T(8,128)S(1)}, f32[128,512]{1,0:T(8,128)S(1)}, u32[]{:S(2)}, u32[]{:S(2)}) collective-permute-start(f32[128,512]{1,0:T(8,128)S(1)} %multiply_add_fusion.8), channel_id=1, source_target_pairs={{0,4},{4,8},{8,12},{12,16},{16,20},{20,24},{24,28},{1,5},{5,9},{9,... | collective-permute-start | bytes 786440 | tf_op jit(solution)/shard_map/while/body/eval_jaxpr/ppermute | solution.py:15
  80.8 59.1 %reduce-scatter.2.cloned.1.call-start = ((), (), s32[]{:S(2)}) async-start(), calls=%async_computation.1 | async-start | bytes 2621440 | tf_op jit(solution)/shard_map/reduce_scatter | solution.py:62
  81.8 2.7 copy-start.6
  84.2 239.7 %all-reduce.6.cloned.1.call-start = ((), (), s32[]{:S(2)}) async-start(), calls=%async_computation.3 | async-start | bytes 4718592 | tf_op jit(solution)/shard_map/psum | solution.py:94
  106.4 3.5 %copy-start.1 = (bf16[2,512,512]{2,1,0:T(8,128)(2,1)S(1)}, bf16[2,512,512]{2,1,0:T(8,128)(2,1)}, u32[]{:S(2)}) copy-start(bf16[2,512,512]{2,1,0:T(8,128)(2,1)} %all-gather.2.cloned.1.call-done) | copy-start | bytes 3145732
  142.7 10.0 %collective-permute-start = (f32[128,512]{1,0:T(8,128)S(1)}, f32[128,512]{1,0:T(8,128)S(1)}, u32[]{:S(2)}, u32[]{:S(2)}) collective-permute-start(f32[128,512]{1,0:T(8,128)S(1)} %multiply_add_fusion.7), channel_id=1, source_target_pairs={{4,0},{8,4},{12,8},{16,12},{20,16},{24,20},{28,24},{5,1},{9,5},{13... | collective-permute-start | bytes 786440 | tf_op jit(solution)/shard_map/while/body/eval_jaxpr/ppermute | solution.py:15
  152.8 9.1 %collective-permute-start = (f32[128,512]{1,0:T(8,128)S(1)}, f32[128,512]{1,0:T(8,128)S(1)}, u32[]{:S(2)}, u32[]{:S(2)}) collective-permute-start(f32[128,512]{1,0:T(8,128)S(1)} %multiply_add_fusion.7), channel_id=1, source_target_pairs={{4,0},{8,4},{12,8},{16,12},{20,16},{24,20},{28,24},{5,1},{9,5},{13... | collective-permute-start | bytes 786440 | tf_op jit(solution)/shard_map/while/body/eval_jaxpr/ppermute | solution.py:15
  161.9 8.0 %collective-permute-start = (f32[128,512]{1,0:T(8,128)S(1)}, f32[128,512]{1,0:T(8,128)S(1)}, u32[]{:S(2)}, u32[]{:S(2)}) collective-permute-start(f32[128,512]{1,0:T(8,128)S(1)} %multiply_add_fusion.7), channel_id=1, source_target_pairs={{4,0},{8,4},{12,8},{16,12},{20,16},{24,20},{28,24},{5,1},{9,5},{13... | collective-permute-start | bytes 786440 | tf_op jit(solution)/shard_map/while/body/eval_jaxpr/ppermute | solution.py:15
  170.1 8.0 %collective-permute-start = (f32[128,512]{1,0:T(8,128)S(1)}, f32[128,512]{1,0:T(8,128)S(1)}, u32[]{:S(2)}, u32[]{:S(2)}) collective-permute-start(f32[128,512]{1,0:T(8,128)S(1)} %multiply_add_fusion.7), channel_id=1, source_target_pairs={{4,0},{8,4},{12,8},{16,12},{20,16},{24,20},{28,24},{5,1},{9,5},{13... | collective-permute-start | bytes 786440 | tf_op jit(solution)/shard_map/while/body/eval_jaxpr/ppermute | solution.py:15
  178.2 8.0 %collective-permute-start = (f32[128,512]{1,0:T(8,128)S(1)}, f32[128,512]{1,0:T(8,128)S(1)}, u32[]{:S(2)}, u32[]{:S(2)}) collective-permute-start(f32[128,512]{1,0:T(8,128)S(1)} %multiply_add_fusion.7), channel_id=1, source_target_pairs={{4,0},{8,4},{12,8},{16,12},{20,16},{24,20},{28,24},{5,1},{9,5},{13... | collective-permute-start | bytes 786440 | tf_op jit(solution)/shard_map/while/body/eval_jaxpr/ppermute | solution.py:15
  186.3 8.0 %collective-permute-start = (f32[128,512]{1,0:T(8,128)S(1)}, f32[128,512]{1,0:T(8,128)S(1)}, u32[]{:S(2)}, u32[]{:S(2)}) collective-permute-start(f32[128,512]{1,0:T(8,128)S(1)} %multiply_add_fusion.7), channel_id=1, source_target_pairs={{4,0},{8,4},{12,8},{16,12},{20,16},{24,20},{28,24},{5,1},{9,5},{13... | collective-permute-start | bytes 786440 | tf_op jit(solution)/shard_map/while/body/eval_jaxpr/ppermute | solution.py:15
  194.4 9.1 %collective-permute-start = (f32[128,512]{1,0:T(8,128)S(1)}, f32[128,512]{1,0:T(8,128)S(1)}, u32[]{:S(2)}, u32[]{:S(2)}) collective-permute-start(f32[128,512]{1,0:T(8,128)S(1)} %multiply_add_fusion.7), channel_id=1, source_target_pairs={{4,0},{8,4},{12,8},{16,12},{20,16},{24,20},{28,24},{5,1},{9,5},{13... | collective-permute-start | bytes 786440 | tf_op jit(solution)/shard_map/while/body/eval_jaxpr/ppermute | solution.py:15
  (1 other events, 1.5 us)
Sparse Core Ops, SparseCore 0:
  80.9 25.3 all-gather.1
  108.9 31.0 reduce-scatter.1
  208.4 115.4 all-reduce.5
where the time goes:
time: 339 us; the launch traced here: 336 us
  waiting for transfers between devices  233 us (69%)
  starting transfers between devices  45.1 us (13%)
  other arithmetic  20.2 us (6%)
  between operations  14.1 us (4%)
  matrix products  12.6 us (4%)
  local copies, waits for them, and re-layouts  9.91 us (3%)
    psum x1, waiting for transfers between devices, body(): grad_b, grad_c = lax.psum((grad_b_part, grad_c_part), 'tm')  115 us
    ppermute x14, waiting for transfers between devices, passed_along(): lax.ppermute(value, axis, [(source, source + steps) for source in range(f...  73.9 us
    ppermute x14, starting transfers between devices, passed_along(): lax.ppermute(value, axis, [(source, source + steps) for source in range(f...  44.8 us
    reduce_scatter x1, waiting for transfers between devices, body(): lax.psum_scatter(jnp.einsum('kup,fkus->pfs', kernel_c, cot_stack, preferr...  22.7 us
    all_gather x1, waiting for transfers between devices, body(): lax.all_gather(states_bf, 'chan', axis=1, tiled=True)  21.7 us
    unnamed x26, other arithmetic  14.4 us
    unnamed x18, local copies, waits for them, and re-layouts  7.18 us
  transfers between devices with their start and end apart: 17, of which 17 were waited for; matrix products, arithmetic and copies ran while one was open for 4% of the time, Pallas kernels for 0%

commit v1 on v0

v1 whole, which is shorter than its diff:
```python
import jax
import jax.numpy as jnp
from jax import lax
from jax.experimental import pallas as pl
from jax.experimental.pallas import tpu as pltpu
from jax.sharding import PartitionSpec as P

W = 64
ROWS = 16
MESH = pl.DeviceIdType.MESH
F32 = jnp.float32
BF16 = jnp.bfloat16

offsets = ((-1, -1), (-1, 0), (-1, 1), (0, -1), (0, 0), (0, 1), (1, -1), (1, 0), (1, 1))


def nt(a, b):
    return lax.dot_general(a, b, (((1,), (1,)), ((), ())), preferred_element_type=F32)


def build_stack(source, stack, sign, block=32):
    frames, channels, cells = source.shape
    blocks = channels // block
    cell = lax.broadcasted_iota(jnp.int32, (1, cells), 1)
    column = cell % W
    masks = []
    for dr, dc in offsets:
        dr, dc = sign * dr, sign * dc
        ok = (column + dc >= 0) & (column + dc < W)
        there = cell + dr * W
        masks.append(ok & (there >= 0) & (there < cells))

    def step(index, carry):
        frame = index // blocks
        row = pl.multiple_of((index % blocks) * block, block)
        lane = pl.multiple_of(frame * cells, cells)
        z = source[frame, pl.ds(row, block), :].astype(F32)
        for k, (dr, dc) in enumerate(offsets):
            by = (-sign * (dr * W + dc)) % cells
            moved = z if by == 0 else pltpu.roll(z, by, 1)
            moved = jnp.where(masks[k], moved, 0.0).astype(BF16)
            stack[pl.ds(pl.multiple_of(k * channels + row, block), block), pl.ds(lane, cells)] = moved
        return carry

    lax.fori_loop(0, frames * blocks, step, 0)


def kernel(n, nc, x_ref, decay_ref, kb_ref, kc_ref, cot_ref,
           gb_out, gc_out, dg_out,
           xs, cs, kbt, kct, kcg, cotg, dr, inj, ent, arr, ebuf, mbuf, erecv, mrecv, eres, mres,
           gcb, gbb, gcrecv, gbrecv, gcred, gbred, gcx,
           cot_s, cot_r, kc_s, kc_r, e_s, e_r, m_s, m_r, ent_s, ent_r, arr_s, arr_r,
           gcs_s, gcs_r, gbs_s, gbs_r, gcx_s, gcx_r, gca_s, gca_r, gba_s, gba_r):
    me = lax.axis_index("tm")
    ch = lax.axis_index("chan")
    frames, channels, cells = x_ref.shape
    taps = kb_ref.shape[0]
    p = kb_ref.shape[1]
    ul = kc_ref.shape[1]
    owners = p // ROWS
    stride = n // owners
    mine = me // stride
    per = gcb.shape[1] // owners
    pending = []

    def on_owner(fn):
        if stride == 1:
            fn()
        else:
            pl.when(lax.rem(me, stride) == 0)(fn)

    def off_owner(fn):
        if stride > 1:
            pl.when(lax.rem(me, stride) != 0)(fn)

    barrier = pltpu.get_barrier_semaphore()
    for d in range(1, n):
        pl.semaphore_signal(barrier, inc=1, device_id={"tm": lax.rem(me + d, n)}, device_id_type=MESH)
    for d in range(1, nc):
        pl.semaphore_signal(barrier, inc=1, device_id={"chan": lax.rem(ch + d, nc)}, device_id_type=MESH)
    pl.semaphore_wait(barrier, n + nc - 2)

    def remote(src, dst, s, r, to):
        return pltpu.make_async_remote_copy(src_ref=src, dst_ref=dst, send_sem=s, recv_sem=r,
                                            device_id=to, device_id_type=MESH)

    def part(ref, c):
        return ref.at[pl.ds(pl.multiple_of(c * ROWS, ROWS), ROWS), :]

    def scatter(piece, recv, s, r):
        for d in range(1, owners):
            c = lax.rem(mine + d, owners)
            to = c * stride
            rel = lax.rem(me - to + n, n) if stride > 1 else n - d
            copy = remote(piece(c), recv.at[rel], s.at[d], r.at[rel], {"tm": to})
            copy.start()
            pending.append((copy, None))

        def near():
            rel = lax.rem(me, stride)
            copy = remote(piece(mine), recv.at[rel], s.at[0], r.at[rel], {"tm": mine * stride})
            copy.start()
            copy.wait_send()

        off_owner(near)

    def arrived(piece, recv, s, r):
        for rel in range(1, n):
            remote(piece(0), recv.at[rel], s.at[0], r.at[rel], {"tm": me}).wait_recv()

    def spread(src, dst, s, r):
        copies = []
        for d in range(1, n):
            copies.append(remote(src, dst(mine), s.at[d], r.at[mine], {"tm": lax.rem(me + d, n)}))
        for copy in copies:
            copy.start()
        return copies

    def spread_wait(src, dst, s, r):
        for d in range(1, owners):
            c = lax.rem(mine + d, owners)
            remote(src, dst(c), s.at[0], r.at[c], {"tm": me}).wait_recv()
        off_owner(lambda: remote(src, dst(mine), s.at[0], r.at[mine], {"tm": me}).wait_recv())

    urow = pl.multiple_of(ch * ul, ul)
    gathers = []
    for d in range(1, nc):
        to = lax.rem(ch + d, nc)
        copy = remote(cot_ref, cotg.at[:, pl.ds(urow, ul), :], cot_s.at[d], cot_r.at[d], {"chan": to})
        copy.start()
        gathers.append(copy)
        cols = pl.ds(pl.multiple_of(to * p, p), p)
        copy = remote(kc_ref.at[:, :, cols], kcg.at[:, pl.ds(urow, ul), :], kc_s.at[d], kc_r.at[d], {"chan": to})
        copy.start()
        gathers.append(copy)
    cotg[:, pl.ds(urow, ul), :] = cot_ref[...]
    kcg[:, pl.ds(urow, ul), :] = kc_ref[:, :, pl.ds(pl.multiple_of(ch * p, p), p)]

    rate = decay_ref[...]
    a0 = jnp.broadcast_to(rate[0:1], (128, p)).T
    a1 = jnp.broadcast_to(rate[1:2], (128, p)).T
    wide = lambda a: jnp.concatenate([a] * (cells // 128), axis=1)

    build_stack(x_ref, xs, 1)
    for k in range(taps):
        kbt[:, k * channels:(k + 1) * channels] = kb_ref[k]
    dr[...] = jnp.dot(kbt[...], xs[...], preferred_element_type=F32)
    ebuf[:, :cells] = wide(a1) * dr[:, :cells] + dr[:, cells:]
    ebuf[:, cells:] = a0 * a1
    scatter(lambda c: part(ebuf, c), erecv, e_s, e_r)

    for copy in gathers:
        copy.wait_recv()
    build_stack(cotg, cs, -1)
    for k in range(taps):
        kct[:, k * channels:(k + 1) * channels] = kcg[k].T

    def scan_forward():
        arrived(lambda c: part(ebuf, c), erecv, e_s, e_r)
        erecv[0] = ebuf[pl.ds(pl.multiple_of(mine * ROWS, ROWS), ROWS), :]
        carried = jnp.zeros((ROWS, cells), F32)
        for j in range(n):
            eres[j] = carried
            if j < n - 1:
                slot = lax.rem(j - me + n, n)
                carried = wide(erecv[slot, :, cells:]) * carried + erecv[slot, :, :cells]

    def scan_backward():
        arrived(lambda c: part(mbuf, c), mrecv, m_s, m_r)
        mrecv[0] = mbuf[pl.ds(pl.multiple_of(mine * ROWS, ROWS), ROWS), :]
        carried = jnp.zeros((ROWS, cells), F32)
        for j in range(n - 1, -1, -1):
            mres[j] = carried
            if j > 0:
                slot = lax.rem(j - me + n, n)
                carried = wide(erecv[slot, :, cells:]) * carried + mrecv[slot]

    def hand_back(res, dst, s, r):
        row = pl.multiple_of(mine * ROWS, ROWS)
        dst[pl.ds(row, ROWS), :] = res[me]
        for d in range(1, n):
            to = lax.rem(me + d, n)
            remote(res.at[to], part(dst, mine), s.at[d], r.at[mine], {"tm": to}).start()

    def handed(res, dst, s, r):
        spread_wait(res.at[0], lambda c: part(dst, c), s, r)

    def drain(src, s):
        for d in range(1, n):
            remote(src, src, s.at[d], s.at[d], {"tm": me}).wait_send()

    def forward():
        scan_forward()
        hand_back(eres, ent, ent_s, ent_r)

    on_owner(forward)

    inj[...] = jnp.dot(kct[...], cs[...], preferred_element_type=F32)
    mbuf[...] = wide(a0) * (inj[:, :cells] + wide(a1) * inj[:, cells:])
    scatter(lambda c: part(mbuf, c), mrecv, m_s, m_r)

    handed(eres, ent, ent_s, ent_r)
    s0 = wide(a0) * ent[...] + dr[:, :cells]
    s1 = wide(a1) * s0 + dr[:, cells:]
    dr[:, :cells] = s0
    states = jnp.concatenate([s0.astype(BF16), s1.astype(BF16)], axis=1)
    units = channels // ROWS // nc
    gcb[:, taps * units:] = jnp.zeros((nc, gcb.shape[1] - taps * units, ROWS, p), BF16)
    for k in range(taps):
        grad = nt(cs[k * channels:(k + 1) * channels, :], states).astype(BF16)
        gcb[:, k * units:(k + 1) * units] = grad.reshape(nc, units, ROWS, p)
    gc_piece = lambda c: gcb.at[:, pl.ds(c * per, per)]
    scatter(gc_piece, gcrecv, gcs_s, gcs_r)

    def backward():
        scan_backward()
        hand_back(mres, arr, arr_s, arr_r)

    on_owner(backward)

    handed(mres, arr, arr_s, arr_r)
    adj1 = inj[:, cells:] + arr[...]
    adj0 = inj[:, :cells] + wide(a1) * adj1
    inj[:, :cells] = adj0
    inj[:, cells:] = adj1
    adjoint = jnp.concatenate([adj0.astype(BF16), adj1.astype(BF16)], axis=1)
    for k in range(taps):
        gbb[k] = nt(adjoint, xs[k * channels:(k + 1) * channels, :]).astype(BF16)
    gb_piece = lambda c: gbb.at[:, pl.ds(pl.multiple_of(c * ROWS, ROWS), ROWS), :]
    scatter(gb_piece, gbrecv, gbs_s, gbs_r)

    gc_slot = lambda c: gc_out.at[:, pl.ds(c * per, per)]
    gb_slot = lambda c: gb_out.at[:, pl.ds(pl.multiple_of(c * ROWS, ROWS), ROWS), :]

    def reduce_gc():
        arrived(gc_piece, gcrecv, gcs_s, gcs_r)
        total = gcb[:, pl.ds(mine * per, per)].astype(F32)
        for rel in range(1, n):
            total = total + gcrecv[rel].astype(F32)
        gcred[...] = total.astype(BF16)
        gcx[ch] = gcred[ch]
        for d in range(1, nc):
            to = lax.rem(ch + d, nc)
            remote(gcred.at[to], gcx.at[ch], gcx_s.at[d], gcx_r.at[d], {"chan": to}).start()

    on_owner(reduce_gc)

    def fold(product):
        lanes = product[:, :128]
        for i in range(1, cells // 128):
            lanes = lanes + product[:, i * 128:(i + 1) * 128]
        return jnp.sum(lanes.T, axis=0, keepdims=True)

    dg_out[0:1, :] = fold(inj[:, :cells] * ent[...])
    dg_out[1:2, :] = fold(inj[:, cells:] * dr[:, :cells])

    def share_gc():
        for d in range(1, nc):
            remote(gcred.at[0], gcx.at[lax.rem(ch - d + nc, nc)], gcx_s.at[d], gcx_r.at[d], {"chan": ch}).wait()
        gc_out[:, pl.ds(mine * per, per)] = gcx[...]
        spread(gcx, gc_slot, gca_s, gca_r)

    on_owner(share_gc)

    def reduce_gb():
        arrived(gb_piece, gbrecv, gbs_s, gbs_r)
        row = pl.ds(pl.multiple_of(mine * ROWS, ROWS), ROWS)
        total = gbb[:, row, :].astype(F32)
        for rel in range(1, n):
            total = total + gbrecv[rel].astype(F32)
        gbred[...] = total.astype(BF16)
        gb_out[:, row, :] = gbred[...]
        spread(gbred, gb_slot, gba_s, gba_r)

    on_owner(reduce_gb)

    spread_wait(gcx, gc_slot, gca_s, gca_r)
    spread_wait(gbred, gb_slot, gba_s, gba_r)
    for copy in gathers:
        copy.wait_send()
    for copy, _ in pending:
        copy.wait_send()

    def owner_drain():
        drain(eres.at[0], ent_s)
        drain(mres.at[0], arr_s)
        drain(gcx, gca_s)
        drain(gbred, gba_s)

    on_owner(owner_drain)


def body(n, nc, inputs, decay, kernel_b, kernel_c, cotangent):
    frames, channels, cells = inputs.shape
    taps, p, _ = kernel_b.shape
    owners = p // ROWS
    units = taps * channels // ROWS // nc
    per = -(-units // owners)
    padded = per * owners
    span = frames * cells
    vm = pltpu.VMEM
    dma = lambda count: pltpu.SemaphoreType.DMA((count,))
    scratch = [
        vm((taps * channels, span), BF16), vm((taps * channels, span), BF16),
        vm((p, taps * channels), BF16), vm((p, taps * channels), BF16),
        vm((taps, channels, p), BF16), vm((frames, channels, cells), BF16),
        vm((p, span), F32), vm((p, span), F32),
        vm((p, cells), F32), vm((p, cells), F32),
        vm((p, cells + 128), F32), vm((p, cells), F32),
        vm((n, ROWS, cells + 128), F32), vm((n, ROWS, cells), F32),
        vm((n, ROWS, cells), F32), vm((n, ROWS, cells), F32),
        vm((nc, padded, ROWS, p), BF16), vm((taps, p, channels), BF16),
        vm((n, nc, per, ROWS, p), BF16), vm((n, taps, ROWS, channels), BF16),
        vm((nc, per, ROWS, p), BF16), vm((taps, ROWS, channels), BF16),
        vm((nc, per, ROWS, p), BF16),
        dma(nc), dma(nc), dma(nc), dma(nc),
        dma(owners), dma(n), dma(owners), dma(n),
        dma(n), dma(owners), dma(n), dma(owners),
        dma(owners), dma(n), dma(owners), dma(n),
        dma(nc), dma(nc),
        dma(n), dma(owners), dma(n), dma(owners),
    ]
    flops = 4 * 2 * p * taps * channels * span
    gb, gc, dg = pl.pallas_call(
        lambda *refs: kernel(n, nc, *refs),
        out_shape=(
            jax.ShapeDtypeStruct((taps, p, channels), BF16),
            jax.ShapeDtypeStruct((nc, padded, ROWS, p), BF16),
            jax.ShapeDtypeStruct(decay.shape, F32),
        ),
        in_specs=[pl.BlockSpec(memory_space=vm)] * 5,
        out_specs=(pl.BlockSpec(memory_space=vm),) * 3,
        scratch_shapes=scratch,
        compiler_params=pltpu.CompilerParams(
            collective_id=0, has_side_effects=True, vmem_limit_bytes=56 * 1024 * 1024
        ),
        cost_estimate=pl.CostEstimate(flops=flops, bytes_accessed=8 * 1024 * 1024, transcendentals=0),
    )(inputs, decay, kernel_b, kernel_c, cotangent)
    grad_c = gc[:, :units].reshape(nc, taps, channels // nc, p).transpose(1, 2, 0, 3)
    grad_c = grad_c.reshape(taps, channels // nc, nc * p).astype(F32)
    return gb.astype(F32), grad_c, dg


def solution(mesh):
    n, nc = mesh.shape["tm"], mesh.shape["chan"]
    in_specs = (
        P("tm", None, None),
        P("tm", "chan"),
        P(None, "chan", None),
        P(None, "chan", None),
        P("tm", "chan", None),
    )
    out_specs = (P(None, "chan", None), P(None, "chan", None), P("tm", "chan"))
    return jax.shard_map(lambda *args: body(n, nc, *args), mesh=mesh, in_specs=in_specs,
                         out_specs=out_specs, check_vma=False)
```

time: 339 us -> 98.2 us (0.29)
  waiting for transfers between devices: 233 us -> 0 us
  Pallas kernels: 0 us -> 93.3 us
  starting transfers between devices: 45.1 us -> 0 us
  other arithmetic: 20.2 us -> 3.42 us
  between operations: 14.1 us -> 0.66 us
  matrix products: 12.6 us -> 0 us
  local copies, waits for them, and re-layouts: 9.91 us -> 0.67 us
    psum x1 -> x0, waiting for transfers between devices: 115 us -> none  [body(): grad_b, grad_c = lax.psum((grad_b_part, grad_c_part), 'tm')]
    pallas_call x0 -> x1, Pallas kernels: none -> 93.3 us  [body(): pl.pallas_call(lambda *refs: kernel(n, nc, *refs), out_shape=(jax.ShapeDt...]
    ppermute x14 -> x0, waiting for transfers between devices: 73.9 us -> none  [passed_along(): lax.ppermute(value, axis, [(source, source + steps) for source in range(f...]
    ppermute x14 -> x0, starting transfers between devices: 44.8 us -> none  [passed_along(): lax.ppermute(value, axis, [(source, source + steps) for source in range(f...]
    reduce_scatter x1 -> x0, waiting for transfers between devices: 22.7 us -> none  [body(): lax.psum_scatter(jnp.einsum('kup,fkus->pfs', kernel_c, cot_stack, preferr...]
    all_gather x1 -> x0, waiting for transfers between devices: 21.7 us -> none  [body(): lax.all_gather(states_bf, 'chan', axis=1, tiled=True)]
    unnamed x26 -> x0, other arithmetic: 14.4 us -> none
    dot_general x4 -> x0, matrix products: 12.6 us -> none  [the longest x1 4.82 us: body(): jnp.einsum('fps,fkcs->kpc', adjoint_bf, input_stack, preferred_element_ty...]
  transfers between devices with their start and end apart: 17 -> 0, of which waited for: 17 -> 0; matrix products, arithmetic and copies ran while one was open for 4% -> 0% of each run, Pallas kernels for 0% -> 0%
where the time goes in v1:
time: 98.2 us; the launch traced here: 98.1 us
  Pallas kernels  93.3 us (95%)
  other arithmetic  3.42 us (3%)
    pallas_call x1, Pallas kernels, body(): pl.pallas_call(lambda *refs: kernel(n, nc, *refs), out_shape=(jax.ShapeDt...  93.3 us
    convert_element_type x1, other arithmetic, body(): return (gb.astype(F32), grad_c, dg)  2.25 us

profile of v1, /device:TPU:15, one launch (start us, length us, event | category | flops | bytes accessed | tf_op | source)
XLA Modules:
  0.0 98.1 jit_solution(1198843828084701374)
XLA Ops:
  0.6 93.3 %shard_map.76 = (bf16[9,128,256]{2,1,0:T(8,128)(2,1)}, bf16[4,40,16,128]{3,2,1,0:T(8,128)(2,1)}, f32[2,128]{1,0:T(2,128)}) custom-call(bf16[2,256,512]{2,1,0:T(8,128)(2,1)} %refs_0_.1, f32[2,128]{1,0:T(2,128)} %refs_1_.1, bf16[9,128,256]{2,1,0:T(8,128)(2,1)} %refs_2_.1, bf16[9,64,512]{2,1,0:T(8,128)(2,1)} %refs_3_.1, bf16[2,64,512]{2,1,0:T(8,128)(2,1)} %refs_4_.1), custom_call_target="tpu_custom_call" | custom-call | flops 2415919104 | bytes 8388608 | tf_op jit(solution)/shard_map/pallas_call | solution.py:324
  94.0 0.0 copy-start
  94.0 2.3 %convert_element_type.15 = f32[9,128,256]{2,1,0:T(8,128)} convert(bf16[9,128,256]{2,1,0:T(8,128)(2,1)} %get-tuple-element.6) | non-fusion elementwise | flops 294912 | bytes 1769472 | tf_op jit(solution)/shard_map/convert_element_type | solution.py:341
  96.2 0.0 copy-done
  96.2 0.1 slice.3
  96.3 0.0 copy-start.1
  96.3 1.2 %copy_bitcast_fusion = f32[9,64,512]{2,1,0:T(8,128)} fusion(bf16[4,9,64,128]{3,2,1,0:T(8,128)(2,1)S(1)} %bitcast.12), kind=kLoop, calls=%fused_computation | loop fusion | flops 294912 | bytes 1769472 | tf_op jit(solution)/shard_map/convert_element_type | solution.py:340
  97.5 0.0 copy-done.1
  97.5 0.6 copy.12
Async XLA Ops:
  94.0 2.3 %copy-start = (bf16[4,40,16,128]{3,2,1,0:T(8,128)(2,1)S(1)}, bf16[4,40,16,128]{3,2,1,0:T(8,128)(2,1)}, u32[]{:S(2)}) copy-start(bf16[4,40,16,128]{3,2,1,0:T(8,128)(2,1)} %get-tuple-element.7) | copy-start | bytes 1966084
  96.3 1.2 %copy-start.1 = (f32[2,128]{1,0:T(2,128)S(1)}, f32[2,128]{1,0:T(2,128)}, u32[]{:S(2)}) copy-start(f32[2,128]{1,0:T(2,128)} %get-tuple-element.14) | copy-start | bytes 3076

commit v2 on v1

--- a/solution.py
+++ b/solution.py
@@ -108,13 +108,32 @@
         for rel in range(1, n):
             remote(piece(0), recv.at[rel], s.at[0], r.at[rel], {"tm": me}).wait_recv()
 
+    staged = stride == 1 and n % 2 == 0 and n > 2
+    beside = me + 1 - 2 * lax.rem(me, 2)
+
     def spread(src, dst, s, r):
-        copies = []
-        for d in range(1, n):
-            copies.append(remote(src, dst(mine), s.at[d], r.at[mine], {"tm": lax.rem(me + d, n)}))
-        for copy in copies:
-            copy.start()
-        return copies
+        if staged:
+            remote(src, dst(mine), s.at[n // 2], r.at[mine], {"tm": beside}).start()
+            for d in range(1, n // 2):
+                remote(src, dst(mine), s.at[d], r.at[mine], {"tm": lax.rem(me + 2 * d, n)}).start()
+        else:
+            for d in range(1, n):
+                remote(src, dst(mine), s.at[d], r.at[mine], {"tm": lax.rem(me + d, n)}).start()
+
+    def pass_on(src, dst, s, r):
+        if staged:
+            for d in range(1, n // 2):
+                c = lax.rem(me - 2 * d + n, n)
+                remote(src, dst(c), s.at[0], r.at[c], {"tm": me}).wait_recv()
+                remote(dst(c), dst(c), s.at[n // 2 + d], r.at[c], {"tm": beside}).start()
+
+    def spread_rest(src, dst, s, r):
+        if staged:
+            for d in range(n // 2):
+                c = lax.rem(beside - 2 * d + n, n)
+                remote(src, dst(c), s.at[0], r.at[c], {"tm": me}).wait_recv()
+        else:
+            spread_wait(src, dst, s, r)
 
     def spread_wait(src, dst, s, r):
         for d in range(1, owners):
@@ -274,8 +293,10 @@
 
     on_owner(reduce_gb)
 
-    spread_wait(gcx, gc_slot, gca_s, gca_r)
-    spread_wait(gbred, gb_slot, gba_s, gba_r)
+    pass_on(gcx, gc_slot, gca_s, gca_r)
+    pass_on(gbred, gb_slot, gba_s, gba_r)
+    spread_rest(gcx, gc_slot, gca_s, gca_r)
+    spread_rest(gbred, gb_slot, gba_s, gba_r)
     for copy in gathers:
         copy.wait_send()
     for copy, _ in pending:

time: 98.2 us -> 92.3 us (0.940)
  the two profiles are of different devices: /device:TPU:15 before, /device:TPU:21 now
where the time goes in v2:
time: 92.3 us; the launch traced here: 92.1 us
  Pallas kernels  87.4 us (95%)
  other arithmetic  3.42 us (4%)
    pallas_call x1, Pallas kernels, body(): pl.pallas_call(lambda *refs: kernel(n, nc, *refs), out_shape=(jax.ShapeDt...  87.4 us
    convert_element_type x1, other arithmetic, body(): return (gb.astype(F32), grad_c, dg)  2.25 us

profile of v2, /device:TPU:21, one launch (start us, length us, event | category | flops | bytes accessed | tf_op | source)
XLA Modules:
  0.0 92.1 jit_solution(11999826188966135727)
XLA Ops:
  0.6 87.4 %shard_map.76 = (bf16[9,128,256]{2,1,0:T(8,128)(2,1)}, bf16[4,40,16,128]{3,2,1,0:T(8,128)(2,1)}, f32[2,128]{1,0:T(2,128)}) custom-call(bf16[2,256,512]{2,1,0:T(8,128)(2,1)} %refs_0_.1, f32[2,128]{1,0:T(2,128)} %refs_1_.1, bf16[9,128,256]{2,1,0:T(8,128)(2,1)} %refs_2_.1, bf16[9,64,512]{2,1,0:T(8,128)(2,1)} %refs_3_.1, bf16[2,64,512]{2,1,0:T(8,128)(2,1)} %refs_4_.1), custom_call_target="tpu_custom_call" | custom-call | flops 2415919104 | bytes 8388608 | tf_op jit(solution)/shard_map/pallas_call | solution.py:345
  88.0 0.0 copy-start
  88.0 2.3 %convert_element_type.15 = f32[9,128,256]{2,1,0:T(8,128)} convert(bf16[9,128,256]{2,1,0:T(8,128)(2,1)} %get-tuple-element.6) | non-fusion elementwise | flops 294912 | bytes 1769472 | tf_op jit(solution)/shard_map/convert_element_type | solution.py:362
  90.3 0.0 copy-done
  90.3 0.1 slice.3
  90.4 0.0 copy-start.1
  90.4 1.2 %copy_bitcast_fusion = f32[9,64,512]{2,1,0:T(8,128)} fusion(bf16[4,9,64,128]{3,2,1,0:T(8,128)(2,1)S(1)} %bitcast.12), kind=kLoop, calls=%fused_computation | loop fusion | flops 294912 | bytes 1769472 | tf_op jit(solution)/shard_map/convert_element_type | solution.py:361
  91.5 0.0 copy-done.1
  91.5 0.6 copy.12
Async XLA Ops:
  88.0 2.3 %copy-start = (bf16[4,40,16,128]{3,2,1,0:T(8,128)(2,1)S(1)}, bf16[4,40,16,128]{3,2,1,0:T(8,128)(2,1)}, u32[]{:S(2)}) copy-start(bf16[4,40,16,128]{3,2,1,0:T(8,128)(2,1)} %get-tuple-element.7) | copy-start | bytes 1966084
  90.4 1.2 %copy-start.1 = (f32[2,128]{1,0:T(2,128)S(1)}, f32[2,128]{1,0:T(2,128)}, u32[]{:S(2)}) copy-start(f32[2,128]{1,0:T(2,128)} %get-tuple-element.14) | copy-start | bytes 3076
